TPU v7x, 32 devices: a whole 2x2x4 slice. The times are simulated.
32 devices in a mesh: py: 8 (over y, x, core), px: 4 (over z).
Axes of the slice: x: 2, y: 2, z: 4, core: 2. Of those that a mesh axis runs over, the one named last changes fastest.
Arguments:
- frames: float32 [32, 512, 512], P(('px', 'py')), may hold values from -6 to 6
- shifts: int32 [32, 2], P(('px', 'py')), may hold values from -8 to 8
- start_basis: float32 [32, 16], replicated, may hold values from -6 to 6
Outputs:
- spatial_components: float32 [16, 512, 512], P(None, 'py', 'px')
- temporal_components: float32 [8, 8, 32, 16], P('py', 'px')
- background: float32 [512, 512], P('py', 'px')
All inputs are finite; a program needn't handle non-finite values.
Results may differ from a plain program's by a relative error of at most 0.0003.
Values sent between devices are 32-bit elements; how exact they have to be, the bound alone decides.
A program may use at most 128 MiB of HBM per device.

v0:
```python
import jax
import jax.numpy as jnp
from jax import lax
from jax.sharding import PartitionSpec as P

PATCH = 64
MARGIN = 8
RANK = 16
ITERS = 6
SHIFT = 8


SHRINK = 0.5
EPSILON = 1e-06
HIGH = lax.Precision.HIGHEST


def with_halo(array, sides, width):
    for axis, dim in sides:
        peers, length = (lax.axis_size(axis), array.shape[dim])
        up = [(i, (i + 1) % peers) for i in range(peers - 1)]
        down = [(j, i) for i, j in up]
        last = lax.slice_in_dim(array, length - width, length, axis=dim)
        first = lax.slice_in_dim(array, 0, width, axis=dim)
        before = lax.ppermute(last, axis, up)
        after = lax.ppermute(first, axis, down)
        array = jnp.concatenate([before, array, after], axis=dim)
    return array


def orthonormal(matrix):
    count = matrix.shape[-1]
    ident = jnp.eye(count, dtype=matrix.dtype)
    result = matrix
    for sweep in range(2):
        gram = jnp.einsum("...tr,...ts->...rs", result, result, precision=HIGH) + EPSILON * ident
        lower = jnp.linalg.cholesky(gram)
        result = lax.linalg.triangular_solve(
            lower, result, left_side=False, lower=True, transpose_a=True
        )
    return result


def spatial_factor(basis, movie, pixel_mean):
    projected = jnp.einsum("...tr,...tk->...rk", basis, movie, precision=HIGH)
    projected = projected - jnp.sum(basis, axis=-2)[..., :, None] * pixel_mean[..., None, :]
    level = SHRINK * jnp.sqrt(jnp.mean(projected * projected, axis=-1, keepdims=True) + EPSILON)
    return projected - jnp.clip(projected, -level, level)


def temporal_update(factor, movie, pixel_mean):
    product = jnp.einsum("...tk,...rk->...tr", movie, factor, precision=HIGH)
    offset = jnp.einsum("...k,...rk->...r", pixel_mean, factor, precision=HIGH)
    return orthonormal(product - offset[..., None, :])


def place_frame(frame, offset):
    padded = jnp.pad(frame, SHIFT)
    row0 = SHIFT - offset[0]
    col0 = SHIFT - offset[1]
    return lax.dynamic_slice(padded, (row0, col0), frame.shape)


def on_device(frames, shifts, start_basis):
    frame_count, height, width = frames.shape
    n_rows = lax.axis_size("py")
    n_cols = lax.axis_size("px")
    row_band = height // n_rows
    col_strip = width // n_cols
    moved = jax.vmap(place_frame)(frames, shifts)
    blocks = moved.reshape(frame_count, n_rows, row_band, n_cols, col_strip)
    tile_rows = blocks.shape[2]
    tile_cols = blocks.shape[4]
    flattened = blocks.transpose(0, 1, 3, 2, 4).reshape(
        frame_count, n_rows * n_cols, tile_rows, tile_cols
    )
    arrived = lax.all_to_all(flattened, ("py", "px"), split_axis=1, concat_axis=0, tiled=True)
    regrouped = arrived.reshape(n_rows, n_cols, frame_count, tile_rows, tile_cols).transpose(
        1, 0, 2, 3, 4
    )
    regrouped = regrouped.reshape(frame_count * n_rows * n_cols, tile_rows, tile_cols)
    extended = with_halo(regrouped, (("py", 1), ("px", 2)), MARGIN)
    total_frames = extended.shape[0]
    edge = PATCH + 2 * MARGIN
    rows_here = row_band // PATCH
    cols_here = col_strip // PATCH
    movie = jnp.stack(
        [
            extended[
                :, row_id * PATCH : row_id * PATCH + edge, col_id * PATCH : col_id * PATCH + edge
            ].reshape(total_frames, edge * edge)
            for row_id in range(rows_here)
            for col_id in range(cols_here)
        ]
    )
    pixel_mean = jnp.mean(movie, axis=-2)
    basis = jnp.broadcast_to(
        orthonormal(start_basis), (movie.shape[0], total_frames, start_basis.shape[1])
    )
    for step in range(ITERS):
        factor = spatial_factor(basis, movie, pixel_mean)
        basis = temporal_update(factor, movie, pixel_mean)
    factor = spatial_factor(basis, movie, pixel_mean)
    factor = factor.reshape(rows_here, cols_here, RANK, edge, edge)[
        ..., MARGIN : MARGIN + PATCH, MARGIN : MARGIN + PATCH
    ]
    spatial = factor.transpose(2, 0, 3, 1, 4).reshape(RANK, row_band, col_strip)
    temporal = basis.reshape(rows_here, cols_here, total_frames, RANK) * jnp.sqrt(
        jnp.float32(total_frames)
    )
    inner_mean = pixel_mean.reshape(rows_here, cols_here, edge, edge)[
        ..., MARGIN : MARGIN + PATCH, MARGIN : MARGIN + PATCH
    ]
    background = inner_mean.transpose(0, 2, 1, 3).reshape(row_band, col_strip)
    return (spatial, temporal, background)


def solution(mesh):
    placed = (P(("px", "py"), None, None), P(("px", "py"), None), P())
    return jax.shard_map(
        on_device,
        mesh=mesh,
        in_specs=placed,
        out_specs=(P(None, "py", "px"), P("py", "px", None, None), P("py", "px")),
        check_vma=False,
    )
```

profile of v0, /device:TPU:0, one launch (start us, length us, event | category | flops | bytes accessed | tf_op | source)
XLA Modules:
  0.0 176.1 jit_solution(2454643998580574975)
XLA Ops:
  7.6 7.3 %all-to-all-start = ((f32[1,32,64,128]{3,2,0,1:T(8,128)}), f32[1,32,64,128]{3,2,0,1:T(8,128)S(1)}, u32[]{:S(2)}, u32[]{:S(2)}) async-start(f32[1,32,64,128]{3,2,0,1:T(8,128)} %bitcast.8), calls=%async_computation | async-start | bytes 2097152 | tf_op jit(solution)/shard_map/all_to_all | solution.py:77
  24.0 16.0 %all-to-all-done = f32[1,32,64,128]{3,2,0,1:T(8,128)S(1)} async-done(((f32[1,32,64,128]{3,2,0,1:T(8,128)}), f32[1,32,64,128]{3,2,0,1:T(8,128)S(1)}, u32[]{:S(2)}, u32[]{:S(2)}) %all-to-all-start) | async-done | bytes 1048608 | tf_op jit(solution)/shard_map/all_to_all | solution.py:77
  40.1 3.5 %collective-permute-start = (f32[32,8,128]{2,1,0:T(8,128)S(1)}, f32[32,8,128]{2,1,0:T(8,128)S(1)}, u32[]{:S(2)}, u32[]{:S(2)}) collective-permute-start(f32[32,8,128]{2,1,0:T(8,128)S(1)} %get-tuple-element.22), channel_id=1, source_target_pairs={{0,4},{4,8},{8,12},{12,16},{16,20},{20,24},{24,28},{1,5},{5,9},{9,... | collective-permute-start | bytes 393224 | tf_op jit(solution)/shard_map/ppermute | solution.py:25
  50.1 2.9 %collective-permute-start.2 = (f32[32,80,8]{1,2,0:T(8,128)S(1)}, f32[32,80,8]{1,2,0:T(8,128)S(1)}, u32[]{:S(2)}, u32[]{:S(2)}) collective-permute-start(f32[32,80,8]{1,2,0:T(8,128)S(1)} %copy.186), channel_id=1, source_target_pairs={{0,1},{1,2},{2,3},{4,5},{5,6},{6,7},{8,9},{9,10},{10,11},{12,13},{... | collective-permute-start | bytes 245768 | tf_op jit(solution)/shard_map/ppermute | solution.py:25
  55.9 4.3 %collective-permute-done.3 = f32[32,80,8]{1,2,0:T(8,128)S(1)} collective-permute-done((f32[32,80,8]{1,2,0:T(8,128)S(1)}, f32[32,80,8]{1,2,0:T(8,128)S(1)}, u32[]{:S(2)}, u32[]{:S(2)}) %collective-permute-start.3) | collective-permute-done | bytes 81952 | tf_op jit(solution)/shard_map/ppermute | solution.py:26
  61.7 3.9 %pad_maximum_fusion = (f32[32,80,80]{2,1,0:T(8,128)}, f32[32,80,80]{2,1,0:T(8,128)}) fusion(f32[32,80,8]{2,1,0:T(8,128)} %copy.189, f32[32,8,128]{2,1,0:T(8,128)S(1)} %collective-permute-done.1, f32[32,64,128]{2,1,0:T(8,128)S(1)} %bitcast.266, f32[32,8,128]{2,1,0:T(8,128)S(1)} %collective-permute-done, f32[32,80,8]{2,1,0:T(8,128)S(1)} %copy.187), kind=kLoop, calls=%fused_computation.8 | loop fusion | flops 1228800 | bytes 3112960 | tf_op jit(solution)/shard_map/concatenate | solution.py:27
  65.6 2.8 %stack_reshape.6 = f32[1,32,6400]{2,1,0:T(8,128)} reshape(f32[32,80,80]{2,1,0:T(8,128)} %get-tuple-element.19) | data formatting | bytes 1638400 | tf_op jit(solution)/shard_map/stack;reshape | solution.py:87
  76.7 3.1 %custom-call.36 = f32[2,16,16]{2,1,0:T(8,128)S(1)} custom-call(f32[2,16,16]{2,1,0:T(8,128)S(1)} %fusion.53), custom_call_target="Cholesky" | custom-call | tf_op jit(solution)/shard_map/jit(cholesky)/cholesky | solution.py:37
  80.0 2.5 %custom-call.37 = f32[2,1,16,16]{2,3,1,0:T(8,128)S(1)} custom-call(f32[2,1,16,16]{3,2,1,0:T(8,128)S(1)} %select_bitcast_fusion.11), custom_call_target="InvertDiagBlocksLowerTriangular" | custom-call | tf_op jit(solution)/shard_map/triangular_solve/custom-call.3 | solution.py:38
  83.0 2.9 %custom-call.38 = f32[2,16,16]{2,1,0:T(8,128)S(1)} custom-call(f32[2,16,16]{2,1,0:T(8,128)S(1)} %fusion.51), custom_call_target="Cholesky" | custom-call | tf_op jit(solution)/shard_map/jit(cholesky)/cholesky | solution.py:37
  86.1 2.5 %custom-call.39 = f32[2,1,16,16]{2,3,1,0:T(8,128)S(1)} custom-call(f32[2,1,16,16]{3,2,1,0:T(8,128)S(1)} %select_bitcast_fusion.10), custom_call_target="InvertDiagBlocksLowerTriangular" | custom-call | tf_op jit(solution)/shard_map/triangular_solve/custom-call.3 | solution.py:38
  93.0 2.9 %custom-call.40 = f32[2,16,16]{2,1,0:T(8,128)S(1)} custom-call(f32[2,16,16]{2,1,0:T(8,128)S(1)} %fusion.49), custom_call_target="Cholesky" | custom-call | tf_op jit(solution)/shard_map/jit(cholesky)/cholesky | solution.py:37
  99.1 2.9 %custom-call.42 = f32[2,16,16]{2,1,0:T(8,128)S(1)} custom-call(f32[2,16,16]{2,1,0:T(8,128)S(1)} %fusion.47), custom_call_target="Cholesky" | custom-call | tf_op jit(solution)/shard_map/jit(cholesky)/cholesky | solution.py:37
  109.1 2.9 %custom-call.44 = f32[2,16,16]{2,1,0:T(8,128)S(1)} custom-call(f32[2,16,16]{2,1,0:T(8,128)S(1)} %fusion.45), custom_call_target="Cholesky" | custom-call | tf_op jit(solution)/shard_map/jit(cholesky)/cholesky | solution.py:37
  115.3 2.9 %custom-call.46 = f32[2,16,16]{2,1,0:T(8,128)S(1)} custom-call(f32[2,16,16]{2,1,0:T(8,128)S(1)} %fusion.43), custom_call_target="Cholesky" | custom-call | tf_op jit(solution)/shard_map/jit(cholesky)/cholesky | solution.py:37
  118.4 2.5 %custom-call.47 = f32[2,1,16,16]{2,3,1,0:T(8,128)S(1)} custom-call(f32[2,1,16,16]{3,2,1,0:T(8,128)S(1)} %select_bitcast_fusion.6), custom_call_target="InvertDiagBlocksLowerTriangular" | custom-call | tf_op jit(solution)/shard_map/triangular_solve/custom-call.3 | solution.py:38
  125.3 3.1 %custom-call.48 = f32[2,16,16]{2,1,0:T(8,128)S(1)} custom-call(f32[2,16,16]{2,1,0:T(8,128)S(1)} %fusion.41), custom_call_target="Cholesky" | custom-call | tf_op jit(solution)/shard_map/jit(cholesky)/cholesky | solution.py:37
  131.6 2.9 %custom-call.50 = f32[2,16,16]{2,1,0:T(8,128)S(1)} custom-call(f32[2,16,16]{2,1,0:T(8,128)S(1)} %fusion.39), custom_call_target="Cholesky" | custom-call | tf_op jit(solution)/shard_map/jit(cholesky)/cholesky | solution.py:37
  141.6 2.9 %custom-call.52 = f32[2,16,16]{2,1,0:T(8,128)S(1)} custom-call(f32[2,16,16]{2,1,0:T(8,128)S(1)} %fusion.37), custom_call_target="Cholesky" | custom-call | tf_op jit(solution)/shard_map/jit(cholesky)/cholesky | solution.py:37
  147.7 2.9 %custom-call.54 = f32[2,16,16]{2,1,0:T(8,128)S(1)} custom-call(f32[2,16,16]{2,1,0:T(8,128)S(1)} %fusion.35), custom_call_target="Cholesky" | custom-call | tf_op jit(solution)/shard_map/jit(cholesky)/cholesky | solution.py:37
  157.7 2.9 %custom-call.56 = f32[2,16,16]{2,1,0:T(8,128)S(1)} custom-call(f32[2,16,16]{2,1,0:T(8,128)S(1)} %fusion.33), custom_call_target="Cholesky" | custom-call | tf_op jit(solution)/shard_map/jit(cholesky)/cholesky | solution.py:37
  160.9 2.5 %custom-call.57 = f32[2,1,16,16]{2,3,1,0:T(8,128)S(1)} custom-call(f32[2,1,16,16]{3,2,1,0:T(8,128)S(1)} %select_bitcast_fusion.1), custom_call_target="InvertDiagBlocksLowerTriangular" | custom-call | tf_op jit(solution)/shard_map/triangular_solve/custom-call.3 | solution.py:38
  163.8 2.9 %custom-call.58 = f32[2,16,16]{2,1,0:T(8,128)S(1)} custom-call(f32[2,16,16]{2,1,0:T(8,128)S(1)} %fusion.31), custom_call_target="Cholesky" | custom-call | tf_op jit(solution)/shard_map/jit(cholesky)/cholesky | solution.py:37
  167.0 2.6 %custom-call.59 = f32[2,1,16,16]{2,3,1,0:T(8,128)S(1)} custom-call(f32[2,1,16,16]{3,2,1,0:T(8,128)S(1)} %select_bitcast_fusion), custom_call_target="InvertDiagBlocksLowerTriangular" | custom-call | tf_op jit(solution)/shard_map/triangular_solve/custom-call.3 | solution.py:38
  (174 shorter events, 83.8 us)
Async XLA Ops:
  0.6 14.3 %copy-start = (f32[32,16]{0,1:T(8,128)S(1)}, f32[32,16]{0,1:T(8,128)}, u32[]{:S(2)}) copy-start(f32[32,16]{0,1:T(8,128)} %param.11) | copy-start | bytes 6148
  7.6 32.4 %all-to-all-start = ((f32[1,32,64,128]{3,2,0,1:T(8,128)}), f32[1,32,64,128]{3,2,0,1:T(8,128)S(1)}, u32[]{:S(2)}, u32[]{:S(2)}) async-start(f32[1,32,64,128]{3,2,0,1:T(8,128)} %bitcast.8), calls=%async_computation | async-start | bytes 2097152 | tf_op jit(solution)/shard_map/all_to_all | solution.py:77
  40.1 4.8 %collective-permute-start = (f32[32,8,128]{2,1,0:T(8,128)S(1)}, f32[32,8,128]{2,1,0:T(8,128)S(1)}, u32[]{:S(2)}, u32[]{:S(2)}) collective-permute-start(f32[32,8,128]{2,1,0:T(8,128)S(1)} %get-tuple-element.22), channel_id=1, source_target_pairs={{0,4},{4,8},{8,12},{12,16},{16,20},{20,24},{24,28},{1,5},{5,9},{9,... | collective-permute-start | bytes 393224 | tf_op jit(solution)/shard_map/ppermute | solution.py:25
  43.6 3.2 %collective-permute-start.1 = (f32[32,8,128]{2,1,0:T(8,128)S(1)}, f32[32,8,128]{2,1,0:T(8,128)S(1)}, u32[]{:S(2)}, u32[]{:S(2)}) collective-permute-start(f32[32,8,128]{2,1,0:T(8,128)S(1)} %get-tuple-element.23), channel_id=1, source_target_pairs={{4,0},{8,4},{12,8},{16,12},{20,16},{24,20},{28,24},{5,1},{9,5},{13... | collective-permute-start | bytes 393224 | tf_op jit(solution)/shard_map/ppermute | solution.py:26
  50.1 5.4 %collective-permute-start.2 = (f32[32,80,8]{1,2,0:T(8,128)S(1)}, f32[32,80,8]{1,2,0:T(8,128)S(1)}, u32[]{:S(2)}, u32[]{:S(2)}) collective-permute-start(f32[32,80,8]{1,2,0:T(8,128)S(1)} %copy.186), channel_id=1, source_target_pairs={{0,1},{1,2},{2,3},{4,5},{5,6},{6,7},{8,9},{9,10},{10,11},{12,13},{... | collective-permute-start | bytes 245768 | tf_op jit(solution)/shard_map/ppermute | solution.py:25
  53.3 6.9 %collective-permute-start.3 = (f32[32,80,8]{1,2,0:T(8,128)S(1)}, f32[32,80,8]{1,2,0:T(8,128)S(1)}, u32[]{:S(2)}, u32[]{:S(2)}) collective-permute-start(f32[32,80,8]{1,2,0:T(8,128)S(1)} %copy.188), channel_id=1, source_target_pairs={{1,0},{2,1},{3,2},{5,4},{6,5},{7,6},{9,8},{10,9},{11,10},{13,12},{... | collective-permute-start | bytes 245768 | tf_op jit(solution)/shard_map/ppermute | solution.py:26
  65.6 4.0 %copy-start.1 = (f32[32,80,80]{2,1,0:T(8,128)S(1)}, f32[32,80,80]{2,1,0:T(8,128)}, u32[]{:S(2)}) copy-start(f32[32,80,80]{2,1,0:T(8,128)} %get-tuple-element.18) | copy-start | bytes 2457604
where the time goes:
time: 179 us; the launch traced here: 176 us
  other arithmetic  81.2 us (45%)
  matrix products  29.9 us (17%)
  waiting for transfers between devices  23.1 us (13%)
  local copies, waits for them, and re-layouts  22.1 us (12%)
  starting transfers between devices  16.2 us (9%)
  between operations  3.59 us (2%)
    another operation x43, other arithmetic, orthonormal(): lower = jnp.linalg.cholesky(gram)  41.6 us
    another operation x29, other arithmetic, orthonormal(): lax.linalg.triangular_solve(lower, result, left_side=False, lower=True, t...  34.4 us
    all_to_all x1, waiting for transfers between devices, on_device(): lax.all_to_all(flattened, ('py', 'px'), split_axis=1, concat_axis=0, tile...  16 us
    dot_general x6, matrix products, temporal_update(): product = jnp.einsum('...tk,...rk->...tr', movie, factor, precision=HIGH)  9.66 us
    dot_general x7, matrix products, spatial_factor(): projected = jnp.einsum('...tr,...tk->...rk', basis, movie, precision=HIGH)  7.43 us
    all_to_all x1, starting transfers between devices, on_device(): lax.all_to_all(flattened, ('py', 'px'), split_axis=1, concat_axis=0, tile...  7.3 us
    dot_general x6, matrix products, temporal_update(): offset = jnp.einsum('...k,...rk->...r', pixel_mean, factor, precision=HIGH)  6.96 us
    ppermute x2, starting transfers between devices, with_halo(): before = lax.ppermute(last, axis, up)  6.32 us
  transfers between devices with their start and end apart: 5, of which 4 were waited for; matrix products, arithmetic and copies ran while one was open for 6% of the time, Pallas kernels for 0%

commit v1 on v0

v1 whole, which is shorter than its diff:
```python
import functools

import jax
import jax.numpy as jnp
from jax import lax
from jax.experimental import pallas as pl
from jax.experimental.pallas import tpu as pltpu
from jax.sharding import PartitionSpec as P

PATCH = 64
MARGIN = 8
RANK = 16
ITERS = 6
SHIFT = 8
EDGE = PATCH + 2 * MARGIN
COLS = 2 * PATCH
CORE = EDGE * COLS
SIDE = EDGE * 2 * MARGIN
PIXELS = CORE + SIDE
CHUNK = SIDE
CHUNKS = PIXELS // CHUNK

SHRINK = 0.5
EPSILON = 1e-06
HIGH = lax.Precision.HIGHEST
NT = (((1,), (1,)), ((), ()))


def halves(value):
    high = value.astype(jnp.bfloat16)
    low = (value - high.astype(jnp.float32)).astype(jnp.bfloat16)
    return high, low


def orthonormal_rows(rows):
    rank = lax.broadcasted_iota(jnp.int32, (RANK, 1), 0)
    eye = (
        lax.broadcasted_iota(jnp.int32, (RANK, RANK), 0)
        == lax.broadcasted_iota(jnp.int32, (RANK, RANK), 1)
    )
    for sweep in range(2):
        grams = [
            lax.dot_general(z, z, NT, precision=HIGH, preferred_element_type=jnp.float32)
            + jnp.where(eye, EPSILON, 0.0)
            for z in rows
        ]
        for j in range(RANK - 1):
            for p in range(len(rows)):
                gram, z = grams[p], rows[p]
                ratio = gram[:, j : j + 1] * (1.0 / gram[j : j + 1, j : j + 1])
                ratio = jnp.where(rank > j, ratio, 0.0)
                grams[p] = gram - ratio * gram[j : j + 1, :]
                rows[p] = z - ratio * z[j : j + 1, :]
        for p in range(len(rows)):
            pivot = jnp.sum(jnp.where(eye, grams[p], 0.0), axis=1, keepdims=True)
            rows[p] = rows[p] * lax.rsqrt(pivot)
    return rows


def decompose_kernel(movie_ref, start_ref, spatial_ref, basis_ref, mean_ref, parts, proj):
    frames = movie_ref.shape[0]
    for c in range(CHUNKS):
        at = pl.ds(c * CHUNK, CHUNK)
        raw = movie_ref[:, at]
        mean = jnp.sum(raw, axis=0, keepdims=True) * (1.0 / frames)
        mean_ref[:, at] = mean
        high, low = halves(raw - mean)
        for part, value in enumerate((high, low, high, low)):
            parts[part * frames : (part + 1) * frames, at] = value

    lane = lax.broadcasted_iota(jnp.int32, (2 * RANK, CHUNK), 1)
    patch = lax.broadcasted_iota(jnp.int32, (2 * RANK, CHUNK), 0) // RANK
    from_left = lane % COLS - patch * (PATCH - MARGIN)
    core_mask = (from_left >= 0) & (from_left < PATCH + MARGIN)
    side_mask = lane % (2 * MARGIN) // MARGIN == patch

    def project(basis):
        high = basis.astype(jnp.bfloat16).astype(jnp.float32)
        low = basis - high
        left = jnp.concatenate([high, high, low, low], axis=1).astype(jnp.bfloat16)
        total = jnp.zeros((2 * RANK, 128), jnp.float32)
        for c in range(CHUNKS):
            at = pl.ds(c * CHUNK, CHUNK)
            value = jnp.dot(left, parts[:, at], preferred_element_type=jnp.float32)
            value = jnp.where(core_mask if c < CHUNKS - 1 else side_mask, value, 0.0)
            proj[:, at] = value
            square = value * value
            for t in range(CHUNK // 128):
                total = total + square[:, t * 128 : (t + 1) * 128]
        power = jnp.sum(total, axis=1, keepdims=True) * (1.0 / (EDGE * EDGE))
        return SHRINK * jnp.sqrt(power + EPSILON)

    def shrunk(level, at):
        value = proj[:, at]
        return value - jnp.clip(value, -level, level)

    def step(_, basis):
        level = project(basis)
        total = jnp.zeros((4 * RANK, 2 * frames), jnp.float32)
        for c in range(CHUNKS):
            at = pl.ds(c * CHUNK, CHUNK)
            factor = jnp.concatenate(halves(shrunk(level, at)), axis=0)
            total = total + lax.dot_general(
                factor, parts[: 2 * frames, at], NT, preferred_element_type=jnp.float32
            )
        total = total[: 2 * RANK] + total[2 * RANK :]
        total = total[:, :frames] + total[:, frames:]
        return jnp.concatenate(orthonormal_rows([total[:RANK], total[RANK:]]), axis=0)

    start = orthonormal_rows([start_ref[...]])[0]
    basis = lax.fori_loop(0, ITERS, step, jnp.concatenate([start, start], axis=0))
    basis_ref[...] = basis
    level = project(basis)
    left_half = lax.broadcasted_iota(jnp.int32, (RANK, COLS), 1) < PATCH
    for row in range(PATCH):
        factor = shrunk(level, pl.ds((row + MARGIN) * COLS, COLS))
        spatial_ref[:, row * COLS : (row + 1) * COLS] = jnp.where(
            left_half, factor[:RANK], factor[RANK:]
        )


def decompose(movie, start):
    frames = movie.shape[0]
    vmem = pl.BlockSpec(memory_space=pltpu.VMEM)
    return pl.pallas_call(
        decompose_kernel,
        out_shape=(
            jax.ShapeDtypeStruct((RANK, PATCH * COLS), jnp.float32),
            jax.ShapeDtypeStruct((2 * RANK, frames), jnp.float32),
            jax.ShapeDtypeStruct((1, PIXELS), jnp.float32),
        ),
        in_specs=[vmem, vmem],
        out_specs=(vmem, vmem, vmem),
        scratch_shapes=[
            pltpu.VMEM((4 * frames, PIXELS), jnp.bfloat16),
            pltpu.VMEM((2 * RANK, PIXELS), jnp.float32),
        ],
        compiler_params=pltpu.CompilerParams(vmem_limit_bytes=48 * 1024 * 1024),
        name="decompose",
    )(movie, start)


def place_frame(frame, offset):
    height, width = frame.shape
    padded = jnp.pad(frame, SHIFT + MARGIN)
    size = (height + 2 * MARGIN, width + 2 * MARGIN)
    moved = lax.dynamic_slice(padded, (SHIFT - offset[0], SHIFT - offset[1]), size)
    row = lax.broadcasted_iota(jnp.int32, size, 0)
    col = lax.broadcasted_iota(jnp.int32, size, 1)
    inside = (row >= MARGIN) & (row < MARGIN + height) & (col >= MARGIN) & (col < MARGIN + width)
    return jnp.where(inside, moved, 0.0)


def blocks_of(frame, n_rows, n_cols):
    tops = [r * PATCH for r in range(n_rows)]
    middle = frame[:, MARGIN : MARGIN + n_cols * COLS]
    core = jnp.stack([middle[t : t + EDGE] for t in tops])
    core = core.reshape(n_rows, EDGE, n_cols, COLS).transpose(2, 0, 1, 3)
    sides = []
    for c in range(n_cols):
        left = frame[:, c * COLS : c * COLS + MARGIN]
        start = MARGIN + (c + 1) * COLS
        both = jnp.concatenate([left, frame[:, start : start + MARGIN]], axis=1)
        sides.append(jnp.stack([both[t : t + EDGE] for t in tops]))
    sides = jnp.stack(sides).reshape(n_cols, n_rows, SIDE // COLS, COLS)
    return jnp.concatenate([core, sides], axis=2)


def on_device(frames, shifts, start_basis):
    n_rows = lax.axis_size("py")
    n_cols = lax.axis_size("px")
    assert frames.shape[1:] == (n_rows * PATCH, n_cols * COLS)
    placed = jax.vmap(place_frame)(frames, shifts)
    blocks = jax.vmap(functools.partial(blocks_of, n_rows=n_rows, n_cols=n_cols))(placed)
    blocks = blocks.reshape(frames.shape[0], n_rows * n_cols, PIXELS // COLS, COLS)
    arrived = lax.all_to_all(blocks, ("px", "py"), split_axis=1, concat_axis=0, tiled=True)
    total_frames = arrived.shape[0]
    movie = arrived.reshape(total_frames, PIXELS)
    spatial, basis, mean = decompose(movie, start_basis.T)
    spatial = spatial.reshape(RANK, PATCH, COLS)
    temporal = basis.reshape(1, 2, RANK, total_frames).transpose(0, 1, 3, 2) * jnp.sqrt(
        jnp.float32(total_frames)
    )
    background = mean[0, MARGIN * COLS : (MARGIN + PATCH) * COLS].reshape(PATCH, COLS)
    return (spatial, temporal, background)


def solution(mesh):
    placed = (P(("px", "py"), None, None), P(("px", "py"), None), P())
    return jax.shard_map(
        on_device,
        mesh=mesh,
        in_specs=placed,
        out_specs=(P(None, "py", "px"), P("py", "px", None, None), P("py", "px")),
        check_vma=False,
    )
```

time: 179 us -> 99 us (0.55); the launches traced: 176 us -> 98.8 us
  other arithmetic: 81.2 us -> 6.37 us
  blocking collectives: 0 us -> 43.3 us
  Pallas kernels: 0 us -> 32.8 us
  matrix products: 29.9 us -> 0 us
  waiting for transfers between devices: 23.1 us -> 0 us
  starting transfers between devices: 16.2 us -> 0 us
  local copies, waits for them, and re-layouts: 22.1 us -> 12.4 us
    another operation x72 -> x1, other arithmetic: 76 us -> 0.02 us  [blocks_of(): sides = jnp.stack(sides).reshape(n_cols, n_rows, SIDE // COLS, COLS)]
    all_to_all x0 -> x1, blocking collectives: none -> 43.3 us  [on_device(): lax.all_to_all(blocks, ('px', 'py'), split_axis=1, concat_axis=0, tiled=T...]
    pallas_call x0 -> x1, Pallas kernels: none -> 32.8 us  [decompose(): pl.pallas_call(decompose_kernel, out_shape=(jax.ShapeDtypeStruct((RANK, P...]
    dot_general x33 -> x0, matrix products: 26.1 us -> none  [the longest x6 9.66 us: temporal_update(): product = jnp.einsum('...tk,...rk->...tr', movie, factor, precision=HIGH)]
    all_to_all x1 -> x0, waiting for transfers between devices: 16 us -> none  [on_device(): lax.all_to_all(flattened, ('py', 'px'), split_axis=1, concat_axis=0, tile...]
    ppermute x4 -> x0, starting transfers between devices: 8.92 us -> none  [the longest x2 6.32 us: with_halo(): before = lax.ppermute(last, axis, up)]
    all_to_all x1 -> x0, starting transfers between devices: 7.3 us -> none  [on_device(): lax.all_to_all(flattened, ('py', 'px'), split_axis=1, concat_axis=0, tile...]
    ppermute x4 -> x0, waiting for transfers between devices: 7.04 us -> none  [the longest x2 6.23 us: with_halo(): after = lax.ppermute(first, axis, down)]
  transfers between devices with their start and end apart: 5 -> 0, of which waited for: 4 -> 0; matrix products, arithmetic and copies ran while one was open for 6% -> 0% of each run, Pallas kernels for 0% -> 0%
where the time goes in v1:
time: 99 us; the launch traced here: 98.8 us
  blocking collectives  43.3 us (44%)
  Pallas kernels  32.8 us (33%)
  local copies, waits for them, and re-layouts  12.4 us (13%)
  other arithmetic  6.37 us (6%)
  between operations  3.89 us (4%)
    all_to_all x1, blocking collectives, on_device(): lax.all_to_all(blocks, ('px', 'py'), split_axis=1, concat_axis=0, tiled=T...  43.3 us
    pallas_call x1, Pallas kernels, decompose(): pl.pallas_call(decompose_kernel, out_shape=(jax.ShapeDtypeStruct((RANK, P...  32.8 us
    unnamed x40, local copies, waits for them, and re-layouts  3.56 us
    all_to_all x1, other arithmetic, on_device(): lax.all_to_all(blocks, ('px', 'py'), split_axis=1, concat_axis=0, tiled=T...  3.51 us
    slice x32, local copies, waits for them, and re-layouts, blocks_of(): sides.append(jnp.stack([both[t:t + EDGE] for t in tops]))  2.81 us
    another operation x36, local copies, waits for them, and re-layouts, blocks_of(): sides.append(jnp.stack([both[t:t + EDGE] for t in tops]))  2.59 us

profile of v1, /device:TPU:0, one launch (start us, length us, event | category | flops | bytes accessed | tf_op | source)
XLA Modules:
  0.0 98.8 jit_solution(6992683110822963421)
XLA Ops:
  0.6 1.3 %fusion.32 = (s32[1,1]{1,0:T(1,128)}, s32[1,1]{1,0:T(1,128)}) fusion(s32[1,2]{1,0:T(1,128)} %param.4), kind=kLoop, calls=%fused_computation.139 | loop fusion | bytes 16 | tf_op jit(solution)/shard_map/vmap()/slice | solution.py:147
  4.6 1.6 %copy.10 = f32[1,512,512]{1,2,0:T(8,128)S(1)} copy(f32[1,512,512]{2,1,0:T(8,128)} %param.3) | data formatting | bytes 2097152 | tf_op args[0]
  6.1 0.6 fusion
  6.8 0.3 fusion.30
  7.2 0.1 copy.26
  7.5 0.1 copy.20
  7.7 0.1 copy.21
  13.4 0.2 copy.51
  13.5 0.1 copy.18
  13.7 0.1 copy.17
  13.8 0.1 copy.16
  13.9 0.1 copy.15
  14.0 0.1 copy.14
  14.2 0.1 copy.13
  14.3 0.1 copy.12
  14.4 0.1 copy.11
  14.8 1.3 %pad_maximum_fusion = f32[1,4,8,90,128]{4,0,3,2,1:T(1,128)S(1)} fusion(f32[1,4,8,10,128]{4,0,3,2,1:T(1,128)S(1)} %copy.51, f32[1,4,8,80,128]{4,0,3,2,1:T(1,128)S(1)} %bitcast.32), kind=kLoop, calls=%fused_computation.1 | loop fusion | flops 368640 | bytes 2949120 | tf_op jit(solution)/shard_map/vmap()/concatenate | solution.py:166
  16.1 43.3 %all_to_all.4 = f32[1,32,90,128]{3,0,2,1:T(1,128)S(1)} all-to-all(f32[1,32,90,128]{3,0,2,1:T(1,128)S(1)} %bitcast.31), channel_id=1, replica_groups=mesh['py'=8,'px'=4] {'px','py'}, dimensions={1} | all-to-all | bytes 2949120 | tf_op jit(solution)/shard_map/all_to_all | solution.py:176
  59.4 3.5 %reduce = f32[32,90,128]{2,1,0:T(8,128)S(1)} reduce(f32[1,32,90,128]{3,0,2,1:T(1,128)S(1)} %all_to_all.4, f32[]{:T(128)} %constant.47), dimensions={0}, to_apply=%all_to_all.2.reduce_sub_computation | reduce | bytes 2949124 | tf_op jit(solution)/shard_map/all_to_all | solution.py:176
  63.0 0.9 copy.55
  63.8 32.8 %decompose.1 = (f32[16,8192]{1,0:T(8,128)S(1)}, f32[32,32]{1,0:T(8,128)S(1)}, f32[1,11520]{1,0:T(1,128)S(1)}) custom-call(f32[32,11520]{1,0:T(8,128)S(1)} %bitcast.27, f32[16,32]{1,0:T(8,128)S(1)} %bitcast.29), custom_call_target="tpu_custom_call" | custom-call | tf_op jit(solution)/shard_map/decompose/pallas_call | solution.py:125
  96.7 0.9 copy.53
  97.6 0.6 broadcast_multiply_fusion
  98.2 0.6 slice.212
  (111 shorter events, 5.8 us)
Async XLA Ops:
  63.0 0.9 copy-start

commit v2 on v1

--- a/solution.py
+++ b/solution.py
@@ -1,5 +1,3 @@
-import functools
-
 import jax
 import jax.numpy as jnp
 from jax import lax
@@ -38,22 +36,37 @@
         lax.broadcasted_iota(jnp.int32, (RANK, RANK), 0)
         == lax.broadcasted_iota(jnp.int32, (RANK, RANK), 1)
     )
+    before = (
+        lax.broadcasted_iota(jnp.int32, (RANK, RANK), 0)
+        == lax.broadcasted_iota(jnp.int32, (RANK, RANK), 1) + 1
+    )
     for sweep in range(2):
         grams = [
             lax.dot_general(z, z, NT, precision=HIGH, preferred_element_type=jnp.float32)
             + jnp.where(eye, EPSILON, 0.0)
             for z in rows
         ]
-        for j in range(RANK - 1):
+        for j in range(0, RANK - 2, 2):
             for p in range(len(rows)):
                 gram, z = grams[p], rows[p]
-                ratio = gram[:, j : j + 1] * (1.0 / gram[j : j + 1, j : j + 1])
-                ratio = jnp.where(rank > j, ratio, 0.0)
-                grams[p] = gram - ratio * gram[j : j + 1, :]
-                rows[p] = z - ratio * z[j : j + 1, :]
+                a = gram[j : j + 1, j : j + 1]
+                b = gram[j : j + 1, j + 1 : j + 2]
+                c = gram[j + 1 : j + 2, j + 1 : j + 2]
+                inverse = 1.0 / (c - b * (b / a))
+                below = rank > j + 1
+                ratio0 = jnp.where(below, gram[:, j : j + 1], 0.0)
+                ratio1 = jnp.where(below, gram[:, j + 1 : j + 2], 0.0)
+                ratio1 = (ratio1 - ratio0 * (b / a)) * inverse
+                ratio0 = ratio0 / a - ratio1 * (b / a)
+                grams[p] = gram - ratio0 * gram[j : j + 1] - ratio1 * gram[j + 1 : j + 2]
+                rows[p] = z - ratio0 * z[j : j + 1] - ratio1 * z[j + 1 : j + 2]
         for p in range(len(rows)):
-            pivot = jnp.sum(jnp.where(eye, grams[p], 0.0), axis=1, keepdims=True)
-            rows[p] = rows[p] * lax.rsqrt(pivot)
+            gram, z = grams[p], rows[p]
+            diagonal = jnp.sum(jnp.where(eye, gram, 0.0), axis=1, keepdims=True)
+            below = jnp.sum(jnp.where(before, gram, 0.0), axis=1, keepdims=True)
+            ratio = jnp.where(rank % 2 == 1, below / pltpu.roll(diagonal, 1, 0), 0.0)
+            pivot = diagonal - ratio * below
+            rows[p] = (z - ratio * pltpu.roll(z, 1, 0)) * lax.rsqrt(pivot)
     return rows
 
 
@@ -61,7 +74,10 @@
     frames = movie_ref.shape[0]
     for c in range(CHUNKS):
         at = pl.ds(c * CHUNK, CHUNK)
-        raw = movie_ref[:, at]
+        first_row = c * (CHUNK // COLS)
+        raw = jnp.concatenate(
+            [movie_ref[:, first_row + i, :] for i in range(CHUNK // COLS)], axis=1
+        )
         mean = jnp.sum(raw, axis=0, keepdims=True) * (1.0 / frames)
         mean_ref[:, at] = mean
         high, low = halves(raw - mean)
@@ -140,43 +156,79 @@
     )(movie, start)
 
 
-def place_frame(frame, offset):
+def place_kernel(shift_ref, frame_ref, out_ref, padded):
+    height, width = frame_ref.shape
+    n_cols, n_rows = out_ref.shape[:2]
+    edge = SHIFT + MARGIN
+    down, right = shift_ref[0], shift_ref[1]
+    padded[:edge] = jnp.zeros((edge, width), jnp.float32)
+    padded[edge : edge + height] = frame_ref[...]
+    padded[edge + height :] = jnp.zeros((padded.shape[0] - edge - height, width), jnp.float32)
+    row = lax.broadcasted_iota(jnp.int32, (EDGE, width), 0)
+    col = lax.broadcasted_iota(jnp.int32, (EDGE, width), 1)
+    from_col = col - right
+    col_inside = (from_col >= 0) & (from_col < width)
+    lane = lax.broadcasted_iota(jnp.int32, (EDGE, COLS), 1)
+    row_in_tile = lax.broadcasted_iota(jnp.int32, (8, COLS), 0)
+    turn = jnp.where(right < 0, right + width, right)
+    ahead = SHIFT - down
+    skip = ahead // 8 * 8
+    lift = (EDGE + 8 - ahead % 8) % (EDGE + 8)
+    nothing = jnp.zeros((EDGE, COLS), jnp.float32)
+    for r in range(n_rows):
+        top = r * PATCH - MARGIN
+        block = padded[pl.ds(pl.multiple_of(r * PATCH + skip, 8), EDGE + 8), :]
+        block = pltpu.roll(block, lift, 0)[:EDGE]
+        inside = col_inside & (row + top >= 0) & (row + top < height)
+        block = jnp.where(inside, pltpu.roll(block, turn, 1), 0.0)
+        tiles = [block[:, c * COLS : (c + 1) * COLS] for c in range(n_cols)]
+        for c in range(n_cols):
+            out_ref[c, r, :EDGE, :] = tiles[c]
+            left = tiles[c - 1] if c > 0 else nothing
+            after = tiles[c + 1] if c + 1 < n_cols else nothing
+            sides = jnp.where(lane >= COLS - MARGIN, left, jnp.where(lane < MARGIN, after, 0.0))
+            group = [
+                pltpu.roll(sides[8 * g : 8 * g + 8], (MARGIN + 2 * MARGIN * g) % COLS, 1)
+                for g in range(EDGE // 8)
+            ]
+            out_ref[c, r, EDGE : EDGE + 8, :] = sum(group[1:8], group[0])
+            rest = group[8] + group[9]
+            spread = jnp.where(row_in_tile % 4 == 0, rest, 0.0)
+            for q in range(1, 4):
+                spread += jnp.where(row_in_tile % 4 == q, pltpu.roll(rest, 32 * q, 1), 0.0)
+            for half in range(2):
+                part = jnp.where(row_in_tile // 4 == half, spread, 0.0)
+                out_ref[c, r, EDGE + 8 + half : EDGE + 9 + half, :] = jnp.sum(
+                    part, axis=0, keepdims=True
+                )
+
+
+def place(frame, shift, n_rows, n_cols):
     height, width = frame.shape
-    padded = jnp.pad(frame, SHIFT + MARGIN)
-    size = (height + 2 * MARGIN, width + 2 * MARGIN)
-    moved = lax.dynamic_slice(padded, (SHIFT - offset[0], SHIFT - offset[1]), size)
-    row = lax.broadcasted_iota(jnp.int32, size, 0)
-    col = lax.broadcasted_iota(jnp.int32, size, 1)
-    inside = (row >= MARGIN) & (row < MARGIN + height) & (col >= MARGIN) & (col < MARGIN + width)
-    return jnp.where(inside, moved, 0.0)
-
-
-def blocks_of(frame, n_rows, n_cols):
-    tops = [r * PATCH for r in range(n_rows)]
-    middle = frame[:, MARGIN : MARGIN + n_cols * COLS]
-    core = jnp.stack([middle[t : t + EDGE] for t in tops])
-    core = core.reshape(n_rows, EDGE, n_cols, COLS).transpose(2, 0, 1, 3)
-    sides = []
-    for c in range(n_cols):
-        left = frame[:, c * COLS : c * COLS + MARGIN]
-        start = MARGIN + (c + 1) * COLS
-        both = jnp.concatenate([left, frame[:, start : start + MARGIN]], axis=1)
-        sides.append(jnp.stack([both[t : t + EDGE] for t in tops]))
-    sides = jnp.stack(sides).reshape(n_cols, n_rows, SIDE // COLS, COLS)
-    return jnp.concatenate([core, sides], axis=2)
+    vmem = pl.BlockSpec(memory_space=pltpu.VMEM)
+    return pl.pallas_call(
+        place_kernel,
+        out_shape=jax.ShapeDtypeStruct((n_cols, n_rows, PIXELS // COLS, COLS), jnp.float32),
+        in_specs=[pl.BlockSpec(memory_space=pltpu.SMEM), vmem],
+        out_specs=vmem,
+        scratch_shapes=[pltpu.VMEM((height + 2 * (SHIFT + MARGIN) + 8, width), jnp.float32)],
+        compiler_params=pltpu.CompilerParams(vmem_limit_bytes=48 * 1024 * 1024),
+        name="place",
+    )(shift, frame)
 
 
 def on_device(frames, shifts, start_basis):
     n_rows = lax.axis_size("py")
     n_cols = lax.axis_size("px")
     assert frames.shape[1:] == (n_rows * PATCH, n_cols * COLS)
-    placed = jax.vmap(place_frame)(frames, shifts)
-    blocks = jax.vmap(functools.partial(blocks_of, n_rows=n_rows, n_cols=n_cols))(placed)
+    blocks = jnp.stack(
+        [place(frames[f], shifts[f], n_rows, n_cols) for f in range(frames.shape[0])]
+    )
     blocks = blocks.reshape(frames.shape[0], n_rows * n_cols, PIXELS // COLS, COLS)
     arrived = lax.all_to_all(blocks, ("px", "py"), split_axis=1, concat_axis=0, tiled=True)
+    arrived = arrived.reshape(-1, PIXELS // COLS, COLS)
     total_frames = arrived.shape[0]
-    movie = arrived.reshape(total_frames, PIXELS)
-    spatial, basis, mean = decompose(movie, start_basis.T)
+    spatial, basis, mean = decompose(arrived, start_basis.T)
     spatial = spatial.reshape(RANK, PATCH, COLS)
     temporal = basis.reshape(1, 2, RANK, total_frames).transpose(0, 1, 3, 2) * jnp.sqrt(
         jnp.float32(total_frames)

time: 99 us -> 107 us (1.081)
  Pallas kernels: 32.8 us -> 56.6 us
  local copies, waits for them, and re-layouts: 12.4 us -> 5.59 us
  other arithmetic: 6.37 us -> 0.61 us
  between operations: 3.89 us -> 0.67 us
    pallas_call x1, Pallas kernels: 32.8 us -> 53.1 us  [decompose(): pl.pallas_call(decompose_kernel, out_shape=(jax.ShapeDtypeStruct((RANK, P...]
    slice x35 -> x0, local copies, waits for them, and re-layouts: 4.48 us -> none  [the longest x32 2.81 us: blocks_of(): sides.append(jnp.stack([both[t:t + EDGE] for t in tops]))]
    all_to_all x1 -> x0, other arithmetic: 3.51 us -> none  [on_device(): lax.all_to_all(blocks, ('px', 'py'), split_axis=1, concat_axis=0, tiled=T...]
    pallas_call x0 -> x1, Pallas kernels: none -> 3.48 us  [place(): pl.pallas_call(place_kernel, out_shape=jax.ShapeDtypeStruct((n_cols, n_ro...]
    another operation x46 -> x1, local copies, waits for them, and re-layouts: 3.71 us -> 1.52 us  [on_device(): blocks.reshape(frames.shape[0], n_rows * n_cols, PIXELS // COLS, COLS)]
    concatenate x5 -> x0, other arithmetic: 1.63 us -> none  [the longest x1 1.32 us: blocks_of(): return jnp.concatenate([core, sides], axis=2)]
    unnamed x40 -> x7, local copies, waits for them, and re-layouts: 3.56 us -> 3.27 us
where the time goes in v2:
time: 107 us
  Pallas kernels  56.6 us (53%)
  blocking collectives  43.3 us (40%)
  local copies, waits for them, and re-layouts  5.59 us (5%)
    pallas_call x1, Pallas kernels, decompose(): pl.pallas_call(decompose_kernel, out_shape=(jax.ShapeDtypeStruct((RANK, P...  53.1 us
    all_to_all x1, blocking collectives, on_device(): lax.all_to_all(blocks, ('px', 'py'), split_axis=1, concat_axis=0, tiled=T...  43.3 us
    pallas_call x1, Pallas kernels, place(): pl.pallas_call(place_kernel, out_shape=jax.ShapeDtypeStruct((n_cols, n_ro...  3.48 us
    unnamed x7, local copies, waits for them, and re-layouts  3.27 us

profile of v2, /device:TPU:0, one launch (start us, length us, event | category | flops | bytes accessed | tf_op | source)
XLA Modules:
  0.0 106.8 jit_solution(18429872608421789048)
XLA Ops:
  0.6 0.0 copy-start
  0.6 1.2 %copy-done = f32[1,512,512]{2,1,0:T(8,128)S(1)} copy-done((f32[1,512,512]{2,1,0:T(8,128)S(1)}, f32[1,512,512]{2,1,0:T(8,128)}, u32[]{:S(2)}) %copy-start) | copy-done | bytes 1048600
  1.9 0.0 copy-start.2
  1.9 0.7 copy-done.2
  2.5 3.5 %place.1 = f32[4,8,90,128]{3,2,1,0:T(8,128)S(1)} custom-call(s32[2]{0:T(128)S(1)} %bitcast.19, f32[512,512]{1,0:T(8,128)S(1)} %bitcast.16), custom_call_target="tpu_custom_call" | custom-call | tf_op jit(solution)/shard_map/place/pallas_call | solution.py:209
  6.0 1.5 %copy.7 = f32[1,32,90,128]{3,0,2,1:T(1,128)S(1)} copy(f32[1,32,90,128]{3,2,1,0:T(8,128)S(1)} %bitcast.15) | data formatting | bytes 2949120 | tf_op jit(solution)/shard_map/reshape;stack | solution.py:227
  7.5 43.3 %all_to_all.4 = f32[1,32,90,128]{3,0,2,1:T(1,128)S(1)} all-to-all(f32[1,32,90,128]{3,0,2,1:T(1,128)S(1)} %copy.7), channel_id=1, replica_groups=mesh['py'=8,'px'=4] {'px','py'}, dimensions={1} | all-to-all | bytes 2949120 | tf_op jit(solution)/shard_map/all_to_all | solution.py:228
  50.9 0.0 copy-start.1
  50.9 0.2 copy.13
  51.1 0.5 copy-done.1
  51.6 53.1 %decompose.1 = (f32[16,8192]{1,0:T(8,128)S(1)}, f32[32,32]{1,0:T(8,128)S(1)}, f32[1,11520]{1,0:T(1,128)S(1)}) custom-call(f32[32,90,128]{2,1,0:T(8,128)S(1)} %bitcast.14, f32[16,32]{1,0:T(8,128)S(1)} %bitcast.18), custom_call_target="tpu_custom_call" | custom-call | tf_op jit(solution)/shard_map/decompose/pallas_call | solution.py:141
  104.7 0.9 copy.11
  105.6 0.6 broadcast_multiply_fusion
  106.2 0.6 slice.3
Async XLA Ops:
  0.6 1.2 %copy-start = (f32[1,512,512]{2,1,0:T(8,128)S(1)}, f32[1,512,512]{2,1,0:T(8,128)}, u32[]{:S(2)}) copy-start(f32[1,512,512]{2,1,0:T(8,128)} %param.3) | copy-start | bytes 3145732
  1.9 0.7 copy-start.2
  50.9 0.7 copy-start.1

commit v3 on v2

--- a/solution.py
+++ b/solution.py
@@ -36,37 +36,22 @@
         lax.broadcasted_iota(jnp.int32, (RANK, RANK), 0)
         == lax.broadcasted_iota(jnp.int32, (RANK, RANK), 1)
     )
-    before = (
-        lax.broadcasted_iota(jnp.int32, (RANK, RANK), 0)
-        == lax.broadcasted_iota(jnp.int32, (RANK, RANK), 1) + 1
-    )
     for sweep in range(2):
         grams = [
             lax.dot_general(z, z, NT, precision=HIGH, preferred_element_type=jnp.float32)
             + jnp.where(eye, EPSILON, 0.0)
             for z in rows
         ]
-        for j in range(0, RANK - 2, 2):
+        for j in range(RANK - 1):
             for p in range(len(rows)):
                 gram, z = grams[p], rows[p]
-                a = gram[j : j + 1, j : j + 1]
-                b = gram[j : j + 1, j + 1 : j + 2]
-                c = gram[j + 1 : j + 2, j + 1 : j + 2]
-                inverse = 1.0 / (c - b * (b / a))
-                below = rank > j + 1
-                ratio0 = jnp.where(below, gram[:, j : j + 1], 0.0)
-                ratio1 = jnp.where(below, gram[:, j + 1 : j + 2], 0.0)
-                ratio1 = (ratio1 - ratio0 * (b / a)) * inverse
-                ratio0 = ratio0 / a - ratio1 * (b / a)
-                grams[p] = gram - ratio0 * gram[j : j + 1] - ratio1 * gram[j + 1 : j + 2]
-                rows[p] = z - ratio0 * z[j : j + 1] - ratio1 * z[j + 1 : j + 2]
+                ratio = gram[:, j : j + 1] * (1.0 / gram[j : j + 1, j : j + 1])
+                ratio = jnp.where(rank > j, ratio, 0.0)
+                grams[p] = gram - ratio * gram[j : j + 1, :]
+                rows[p] = z - ratio * z[j : j + 1, :]
         for p in range(len(rows)):
-            gram, z = grams[p], rows[p]
-            diagonal = jnp.sum(jnp.where(eye, gram, 0.0), axis=1, keepdims=True)
-            below = jnp.sum(jnp.where(before, gram, 0.0), axis=1, keepdims=True)
-            ratio = jnp.where(rank % 2 == 1, below / pltpu.roll(diagonal, 1, 0), 0.0)
-            pivot = diagonal - ratio * below
-            rows[p] = (z - ratio * pltpu.roll(z, 1, 0)) * lax.rsqrt(pivot)
+            pivot = jnp.sum(jnp.where(eye, grams[p], 0.0), axis=1, keepdims=True)
+            rows[p] = rows[p] * lax.rsqrt(pivot)
     return rows
 
 

time: 107 us -> 87.7 us (0.82)
  Pallas kernels: 56.6 us -> 37.2 us
    pallas_call x1, Pallas kernels: 53.1 us -> 33.7 us  [decompose(): pl.pallas_call(decompose_kernel, out_shape=(jax.ShapeDtypeStruct((RANK, P...]
where the time goes in v3:
time: 87.7 us; the launch traced here: 87.4 us
  blocking collectives  43.3 us (49%)
  Pallas kernels  37.2 us (42%)
  local copies, waits for them, and re-layouts  5.59 us (6%)
    all_to_all x1, blocking collectives, on_device(): lax.all_to_all(blocks, ('px', 'py'), split_axis=1, concat_axis=0, tiled=T...  43.3 us
    pallas_call x1, Pallas kernels, decompose(): pl.pallas_call(decompose_kernel, out_shape=(jax.ShapeDtypeStruct((RANK, P...  33.7 us
    pallas_call x1, Pallas kernels, place(): pl.pallas_call(place_kernel, out_shape=jax.ShapeDtypeStruct((n_cols, n_ro...  3.48 us
    unnamed x7, local copies, waits for them, and re-layouts  3.27 us

profile of v3, /device:TPU:0, one launch (start us, length us, event | category | flops | bytes accessed | tf_op | source)
XLA Modules:
  0.0 87.4 jit_solution(1900491053942647048)
XLA Ops:
  0.6 0.0 copy-start
  0.6 1.2 %copy-done = f32[1,512,512]{2,1,0:T(8,128)S(1)} copy-done((f32[1,512,512]{2,1,0:T(8,128)S(1)}, f32[1,512,512]{2,1,0:T(8,128)}, u32[]{:S(2)}) %copy-start) | copy-done | bytes 1048600
  1.9 0.0 copy-start.2
  1.9 0.7 copy-done.2
  2.5 3.5 %place.1 = f32[4,8,90,128]{3,2,1,0:T(8,128)S(1)} custom-call(s32[2]{0:T(128)S(1)} %bitcast.19, f32[512,512]{1,0:T(8,128)S(1)} %bitcast.16), custom_call_target="tpu_custom_call" | custom-call | tf_op jit(solution)/shard_map/place/pallas_call | solution.py:194
  6.0 1.5 %copy.7 = f32[1,32,90,128]{3,0,2,1:T(1,128)S(1)} copy(f32[1,32,90,128]{3,2,1,0:T(8,128)S(1)} %bitcast.15) | data formatting | bytes 2949120 | tf_op jit(solution)/shard_map/reshape;stack | solution.py:212
  7.5 43.3 %all_to_all.4 = f32[1,32,90,128]{3,0,2,1:T(1,128)S(1)} all-to-all(f32[1,32,90,128]{3,0,2,1:T(1,128)S(1)} %copy.7), channel_id=1, replica_groups=mesh['py'=8,'px'=4] {'px','py'}, dimensions={1} | all-to-all | bytes 2949120 | tf_op jit(solution)/shard_map/all_to_all | solution.py:213
  50.9 0.0 copy-start.1
  50.9 0.2 copy.13
  51.1 0.5 copy-done.1
  51.6 33.7 %decompose.1 = (f32[16,8192]{1,0:T(8,128)S(1)}, f32[32,32]{1,0:T(8,128)S(1)}, f32[1,11520]{1,0:T(1,128)S(1)}) custom-call(f32[32,90,128]{2,1,0:T(8,128)S(1)} %bitcast.14, f32[16,32]{1,0:T(8,128)S(1)} %bitcast.18), custom_call_target="tpu_custom_call" | custom-call | tf_op jit(solution)/shard_map/decompose/pallas_call | solution.py:126
  85.3 0.9 %copy.11 = f32[2,8,64,128]{3,2,1,0:T(8,128)} copy(f32[2,8,64,128]{3,1,2,0:T(8,128)S(1)} %bitcast.17) | data formatting | bytes 1048576
  86.2 0.6 broadcast_multiply_fusion
  86.8 0.6 slice.3
Async XLA Ops:
  0.6 1.2 %copy-start = (f32[1,512,512]{2,1,0:T(8,128)S(1)}, f32[1,512,512]{2,1,0:T(8,128)}, u32[]{:S(2)}) copy-start(f32[1,512,512]{2,1,0:T(8,128)} %param.3) | copy-start | bytes 3145732
  1.9 0.7 copy-start.2
  50.9 0.7 copy-start.1

commit v4 on v3

--- a/solution.py
+++ b/solution.py
@@ -42,16 +42,17 @@
             + jnp.where(eye, EPSILON, 0.0)
             for z in rows
         ]
-        for j in range(RANK - 1):
-            for p in range(len(rows)):
-                gram, z = grams[p], rows[p]
-                ratio = gram[:, j : j + 1] * (1.0 / gram[j : j + 1, j : j + 1])
-                ratio = jnp.where(rank > j, ratio, 0.0)
-                grams[p] = gram - ratio * gram[j : j + 1, :]
-                rows[p] = z - ratio * z[j : j + 1, :]
         for p in range(len(rows)):
-            pivot = jnp.sum(jnp.where(eye, grams[p], 0.0), axis=1, keepdims=True)
-            rows[p] = rows[p] * lax.rsqrt(pivot)
+            z, gram = rows[p], grams[p]
+            columns = [jnp.broadcast_to(gram[:, m : m + 1], z.shape) for m in range(RANK)]
+            pivots = jnp.zeros_like(z)
+            for j in range(RANK):
+                pivots = jnp.where(rank == j, columns[j], pivots)
+                ratio = jnp.where(rank > j, columns[j], 0.0) * (1.0 / columns[j][j : j + 1])
+                for m in range(j + 1, RANK):
+                    columns[m] = columns[m] - ratio * columns[m][j : j + 1]
+                z = z - ratio * z[j : j + 1]
+            rows[p] = z * lax.rsqrt(pivots)
     return rows
 
 

time: 87.7 us -> 74.6 us (0.85)
  Pallas kernels: 37.2 us -> 24.1 us
    pallas_call x1, Pallas kernels: 33.7 us -> 20.6 us  [decompose(): pl.pallas_call(decompose_kernel, out_shape=(jax.ShapeDtypeStruct((RANK, P...]
where the time goes in v4:
time: 74.6 us; the launch traced here: 74.3 us
  blocking collectives  43.3 us (58%)
  Pallas kernels  24.1 us (32%)
  local copies, waits for them, and re-layouts  5.59 us (7%)
    all_to_all x1, blocking collectives, on_device(): lax.all_to_all(blocks, ('px', 'py'), split_axis=1, concat_axis=0, tiled=T...  43.3 us
    pallas_call x1, Pallas kernels, decompose(): pl.pallas_call(decompose_kernel, out_shape=(jax.ShapeDtypeStruct((RANK, P...  20.6 us
    pallas_call x1, Pallas kernels, place(): pl.pallas_call(place_kernel, out_shape=jax.ShapeDtypeStruct((n_cols, n_ro...  3.48 us
    unnamed x7, local copies, waits for them, and re-layouts  3.27 us
    another operation x1, local copies, waits for them, and re-layouts, on_device(): blocks.reshape(frames.shape[0], n_rows * n_cols, PIXELS // COLS, COLS)  1.52 us

profile of v4, /device:TPU:0, one launch (start us, length us, event | category | flops | bytes accessed | tf_op | source)
XLA Modules:
  0.0 74.3 jit_solution(12531636722047746479)
XLA Ops:
  0.6 0.0 copy-start
  0.6 1.2 %copy-done = f32[1,512,512]{2,1,0:T(8,128)S(1)} copy-done((f32[1,512,512]{2,1,0:T(8,128)S(1)}, f32[1,512,512]{2,1,0:T(8,128)}, u32[]{:S(2)}) %copy-start) | copy-done | bytes 1048600
  1.9 0.0 copy-start.2
  1.9 0.7 copy-done.2
  2.5 3.5 %place.1 = f32[4,8,90,128]{3,2,1,0:T(8,128)S(1)} custom-call(s32[2]{0:T(128)S(1)} %bitcast.19, f32[512,512]{1,0:T(8,128)S(1)} %bitcast.16), custom_call_target="tpu_custom_call" | custom-call | tf_op jit(solution)/shard_map/place/pallas_call | solution.py:195
  6.0 1.5 %copy.7 = f32[1,32,90,128]{3,0,2,1:T(1,128)S(1)} copy(f32[1,32,90,128]{3,2,1,0:T(8,128)S(1)} %bitcast.15) | data formatting | bytes 2949120 | tf_op jit(solution)/shard_map/reshape;stack | solution.py:213
  7.5 43.3 %all_to_all.4 = f32[1,32,90,128]{3,0,2,1:T(1,128)S(1)} all-to-all(f32[1,32,90,128]{3,0,2,1:T(1,128)S(1)} %copy.7), channel_id=1, replica_groups=mesh['py'=8,'px'=4] {'px','py'}, dimensions={1} | all-to-all | bytes 2949120 | tf_op jit(solution)/shard_map/all_to_all | solution.py:214
  50.9 0.0 copy-start.1
  50.9 0.2 copy.13
  51.1 0.5 copy-done.1
  51.6 20.6 %decompose.1 = (f32[16,8192]{1,0:T(8,128)S(1)}, f32[32,32]{1,0:T(8,128)S(1)}, f32[1,11520]{1,0:T(1,128)S(1)}) custom-call(f32[32,90,128]{2,1,0:T(8,128)S(1)} %bitcast.14, f32[16,32]{1,0:T(8,128)S(1)} %bitcast.18), custom_call_target="tpu_custom_call" | custom-call | tf_op jit(solution)/shard_map/decompose/pallas_call | solution.py:127
  72.2 0.9 %copy.11 = f32[2,8,64,128]{3,2,1,0:T(8,128)} copy(f32[2,8,64,128]{3,1,2,0:T(8,128)S(1)} %bitcast.17) | data formatting | bytes 1048576
  73.1 0.6 broadcast_multiply_fusion
  73.7 0.6 slice.3
Async XLA Ops:
  0.6 1.2 %copy-start = (f32[1,512,512]{2,1,0:T(8,128)S(1)}, f32[1,512,512]{2,1,0:T(8,128)}, u32[]{:S(2)}) copy-start(f32[1,512,512]{2,1,0:T(8,128)} %param.3) | copy-start | bytes 3145732
  1.9 0.7 copy-start.2
  50.9 0.7 copy-start.1
